TPU v7x, 768 devices: a whole 4x8x12 slice. The times are simulated.
768 devices in a mesh: sfc: 384 (over z, y, x), grp: 2 (over core).
Axes of the slice: x: 4, y: 8, z: 12, core: 2. Of those that a mesh axis runs over, the one named last changes fastest.
Arguments:
- ocean_field: float32 [16, 1572864], P(None, ('sfc', 'grp')), may hold values from -6 to 6
- atm_field: float32 [16, 1572864], P('grp', 'sfc'), may hold values from -6 to 6
- tile_weights: float32 [18432, 64, 128], P(('sfc', 'grp')), may hold values from -0.75 to 0.75
- tile_source: int32 [18432], P(('sfc', 'grp')), may hold values from 0 to 31
- tile_target: int32 [18432], P(('sfc', 'grp')), may hold values from 0 to 95, as said below
- tile_count: int32 [768], P(('sfc', 'grp')), may hold values from 12 to 24, as said below
- ocean_adjacency: int32 [2, 1572864], P(None, ('sfc', 'grp')), may hold values from 0 to 2047
- atm_adjacency: int32 [2, 1572864], P(None, 'sfc'), may hold values from 0 to 4095
Outputs:
- atm_from_ocean: float32 [16, 1572864], P('grp', 'sfc')
- ocean_from_atm: float32 [16, 1572864], P(None, ('sfc', 'grp'))
Inputs may be any that keep to these rules, and one draw needn't show every extreme that they name: `tile_count`: every device has 12 or more live tiles, and some device has exactly 24. `tile_target`: the tiles of a device with grp index g target blocks from a run of max(2, 2 * 4096 // 64 // 2) blocks that starts at g * 64 // 2; each device's first tile slot targets the last block of its run.
All inputs are finite; a program needn't handle non-finite values.
Results may differ from a plain program's by a relative error of at most 0.0003.
Values sent between devices are 32-bit elements; how exact they have to be, the bound alone decides.
A program may use at most 32 MiB of HBM per device.

v0:
```python
import jax
import jax.numpy as jnp
from jax import lax
from jax.sharding import PartitionSpec as P

TB = 64


HIGH = lax.Precision.HIGHEST


def from_behind(array, axis, by):
    count = lax.axis_size(axis)
    pairs = [(i, i + by) for i in range(count) if 0 <= i + by < count]
    return lax.ppermute(array, axis, pairs)


def curve_slope(field, adjacency):
    ahead = jnp.take(field, adjacency[1], axis=1)
    behind = jnp.take(field, adjacency[0], axis=1)
    return ahead - behind


def per_device(
    ocean_field,
    atm_field,
    tile_weights,
    tile_source,
    tile_target,
    tile_count,
    ocean_adjacency,
    atm_adjacency,
):
    columns_all = ocean_field.shape[0]
    ocean_cells = ocean_field.shape[1]
    atm_cells = atm_field.shape[1]
    slot_total = tile_source.shape[0]
    ocean_blocks = ocean_cells // TB
    window_blocks = 2 * atm_cells // TB
    live_mask = (jnp.arange(slot_total, dtype=jnp.int32) < tile_count[0]).astype(jnp.float32)
    block_ids = jnp.arange(window_blocks, dtype=jnp.int32)
    ocean_slope = curve_slope(ocean_field, ocean_adjacency)
    picked = ocean_field.reshape(columns_all, ocean_blocks, TB)[:, tile_source]
    picked_slope = ocean_slope.reshape(columns_all, ocean_blocks, TB)[:, tile_source]
    joined = jnp.concatenate([picked, picked_slope], axis=2)
    contrib = (
        jnp.einsum("tik,ctk->cti", tile_weights, joined, precision=HIGH) * live_mask[None, :, None]
    )
    target_hot = (tile_target[:, None] == block_ids[None]).astype(jnp.float32)
    partial_value = jnp.einsum("cti,tb->cbi", contrib, target_hot, precision=HIGH).reshape(
        columns_all, 2 * atm_cells
    )
    incoming = from_behind(partial_value[:, atm_cells:], "sfc", 1)
    own_part = partial_value[:, :atm_cells] + incoming
    atm_from_ocean = lax.psum_scatter(own_part, "grp", scatter_dimension=0, tiled=True)
    atm_slope = curve_slope(atm_field, atm_adjacency)
    paired = jnp.stack([atm_field, atm_slope])
    gathered = lax.all_gather(paired, "grp", axis=1, tiled=True)
    following = from_behind(gathered, "sfc", -1)
    window = jnp.concatenate([gathered, following], axis=2)
    shaped = window.reshape(2, columns_all, window_blocks, TB)
    back_terms = jnp.einsum(
        "tij,cti->ctj", tile_weights[:, :, :TB], shaped[0][:, tile_target], precision=HIGH
    ) + jnp.einsum(
        "tij,cti->ctj", tile_weights[:, :, TB:], shaped[1][:, tile_target], precision=HIGH
    )
    source_hot = (tile_source[:, None] == jnp.arange(ocean_blocks, dtype=jnp.int32)[None]).astype(
        jnp.float32
    ) * live_mask[:, None]
    ocean_from_atm = jnp.einsum("ctj,to->coj", back_terms, source_hot, precision=HIGH).reshape(
        columns_all, ocean_cells
    )
    return (atm_from_ocean, ocean_from_atm)


def solution(mesh):
    return jax.shard_map(
        per_device,
        mesh=mesh,
        in_specs=(
            P(None, ("sfc", "grp")),
            P("grp", "sfc"),
            P(("sfc", "grp"), None, None),
            P(("sfc", "grp")),
            P(("sfc", "grp")),
            P(("sfc", "grp")),
            P(None, ("sfc", "grp")),
            P(None, "sfc"),
        ),
        out_specs=(P("grp", "sfc"), P(None, ("sfc", "grp"))),
        check_vma=False,
    )
```

profile of v0, /device:TPU:1, one launch (start us, length us, event | category | flops | bytes accessed | tf_op | source)
XLA Modules:
  0.0 122.0 jit_solution(1061825010798372244)
XLA Ops:
  7.2 0.8 fusion.30
  8.1 1.2 %copy.72 = f32[16,2048]{0,1:T(8,128)S(1)} copy(f32[16,2048]{1,0:T(8,128)} %param.12) | data formatting | bytes 262144 | tf_op args[0]
  9.3 1.0 reshape.43
  12.3 5.5 %gather_fusion.4 = f32[2048,16]{1,0:T(8,128)S(1)} fusion(f32[16,2048]{0,1:T(8,128)S(1)} %copy.72, s32[2048]{0:T(1024)S(1)} %fusion.19), kind=kCustom, calls=%fused_computation.clone | custom fusion | bytes 270336 | tf_op jit(solution)/shard_map/jit(_take)/gather | solution.py:19
  17.8 7.6 %gather_fusion.5 = f32[2048,16]{1,0:T(8,128)} fusion(f32[16,2048]{0,1:T(8,128)S(1)} %copy.72, s32[2048]{0:T(1024)S(1)} %fusion.20), kind=kCustom, calls=%fused_computation.2.clone | custom fusion | bytes 270336 | tf_op jit(solution)/shard_map/jit(_take)/gather | solution.py:20
  25.4 2.9 %bitcast_subtract_fusion.1 = f32[16,2048]{0,1:T(8,128)S(1)} fusion(f32[2048,16]{1,0:T(8,128)} %gather_fusion.5, f32[2048,16]{1,0:T(8,128)S(1)} %gather_fusion.4, pred[2048]{0:T(1024)(128)(4,1)S(1)} %get-tuple-element.12, pred[2048]{0:T(1024)(128)(4,1)S(1)} %get-tuple-element.13), kind=kLoop, calls=%fused_computation.17 | loop fusion | flops 98304 | bytes 397312 | tf_op jit(solution)/shard_map/sub | solution.py:21
  30.5 1.4 %fusion.2 = f32[16,24,64]{2,0,1:T(8,128)S(1)} fusion(f32[24,64,128]{2,1,0:T(8,128)S(1)} %copy-done, f32[16,24,64]{2,0,1:T(8,128)S(1)} %bitcast.46, f32[16,24,64]{2,0,1:T(8,128)S(1)} %bitcast.47, f32[24]{0:T(128)S(1)} %compare_convert_fusion), kind=kOutput, calls=%fused_computation.16 | convolution fusion | flops 37822464 | bytes 1081440 | tf_op jit(solution)/shard_map/tik,ctk->cti/dot_general | solution.py:47
  33.3 0.7 slice.59
  34.0 4.7 %collective-permute-start = (f32[16,4096]{1,0:T(8,128)}, f32[16,4096]{1,0:T(8,128)}, u32[]{:S(2)}, u32[]{:S(2)}) collective-permute-start(f32[16,4096]{1,0:T(8,128)} %slice.59), channel_id=1, source_target_pairs={{0,2},{2,4},{4,6},{6,8},{8,10},{10,12},{12,14},{14,16},{16,18},{18... | collective-permute-start | bytes 786440 | tf_op jit(solution)/shard_map/ppermute | solution.py:15
  40.6 14.2 %gather_fusion.6 = f32[4096,8]{1,0:T(8,128)} fusion(f32[8,4096]{0,1:T(8,128)S(1)} %copy.77, s32[4096]{0:T(1024)S(1)} %fusion.13), kind=kCustom, calls=%fused_computation.1.clone | custom fusion | bytes 278528 | tf_op jit(solution)/shard_map/jit(_take)/gather | solution.py:19
  54.7 15.5 %gather_fusion.7 = f32[4096,8]{1,0:T(8,128)} fusion(f32[8,4096]{0,1:T(8,128)S(1)} %copy.77, s32[4096]{0:T(1024)} %fusion.14), kind=kCustom, calls=%fused_computation.3.clone | custom fusion | bytes 278528 | tf_op jit(solution)/shard_map/jit(_take)/gather | solution.py:20
  70.2 5.1 %fusion = f32[1,8,4096]{1,2,0:T(8,128)S(1)} fusion(f32[4096,8]{1,0:T(8,128)} %gather_fusion.7, f32[4096,8]{1,0:T(8,128)} %gather_fusion.6, pred[4096]{0:T(1024)(128)(4,1)S(1)} %copy-done.3, pred[4096]{0:T(1024)(128)(4,1)S(1)} %copy-done.4), kind=kLoop, calls=%fused_computation.10 | loop fusion | flops 98304 | bytes 401408 | tf_op jit(solution)/shard_map/stack | solution.py:57
  75.4 2.2 %pad_maximum_fusion = f32[2,8,4096]{1,2,0:T(8,128)} fusion(f32[1,8,4096]{1,2,0:T(8,128)S(1)} %fusion, f32[1,8,4096]{1,2,0:T(8,128)S(1)} %bitcast.44), kind=kLoop, calls=%fused_computation.8 | loop fusion | flops 65536 | bytes 524288 | tf_op jit(solution)/shard_map/stack | solution.py:57
  77.6 2.8 %copy.80 = f32[2,8,4096]{2,0,1:T(2,128)S(1)} copy(f32[2,8,4096]{1,2,0:T(8,128)} %pad_maximum_fusion) | data formatting | bytes 524288 | tf_op jit(solution)/shard_map/stack | solution.py:57
  80.4 9.7 %all_gather.3 = f32[2,16,4096]{2,0,1:T(2,128)S(1)} all-gather(f32[2,8,4096]{2,0,1:T(2,128)S(1)} %copy.80), channel_id=1, replica_groups=mesh['sfc'=384,'grp'=2] {'grp'}, dimensions={1}, use_global_device_ids=true | all-gather | bytes 786432 | tf_op jit(solution)/shard_map/all_gather | solution.py:58
  90.4 1.3 %collective-permute-start.1 = (f32[2,16,4096]{2,1,0:T(8,128)S(1)}, f32[2,16,4096]{2,1,0:T(8,128)S(1)}, u32[]{:S(2)}, u32[]{:S(2)}) collective-permute-start(f32[2,16,4096]{2,1,0:T(8,128)S(1)} %get-tuple-element.6), channel_id=1, source_target_pairs={{2,0},{4,2},{6,4},{8,6},{10,8},{12,10},{14,12},{16,14},{18,16},{20... | collective-permute-start | bytes 1572872 | tf_op jit(solution)/shard_map/ppermute | solution.py:15
  91.7 1.7 %slice_add_fusion = f32[16,4096]{1,0:T(8,128)} fusion(f32[16,4096]{1,0:T(8,128)} %collective-permute-done, f32[16,8192]{1,0:T(8,128)S(1)} %reshape.45), kind=kLoop, calls=%fused_computation.21 | loop fusion | flops 65536 | bytes 786432 | tf_op jit(solution)/shard_map/add | solution.py:54
  93.4 12.0 %collective-permute-done.1 = f32[2,16,4096]{2,1,0:T(8,128)S(1)} collective-permute-done((f32[2,16,4096]{2,1,0:T(8,128)S(1)}, f32[2,16,4096]{2,1,0:T(8,128)S(1)}, u32[]{:S(2)}, u32[]{:S(2)}) %collective-permute-start.1) | collective-permute-done | bytes 524320 | tf_op jit(solution)/shard_map/ppermute | solution.py:15
  106.6 0.7 gather_fusion.2
  107.3 0.8 fusion.4
  109.1 0.7 gather_fusion.3
  109.8 0.9 fusion.1
  111.3 0.8 reshape.46
  112.0 3.1 %reduce-scatter.2.cloned.1.call-done = f32[8,4096]{1,0:T(8,128)} async-done(((f32[16,4096]{1,0:T(8,128)}), f32[8,4096]{1,0:T(8,128)}) %reduce-scatter.2.cloned.1.call-update) | async-done | bytes 131088 | tf_op jit(solution)/shard_map/reduce_scatter | solution.py:55
  (48 shorter events, 9.8 us)
Async XLA Ops:
  7.2 108.0 %reduce-scatter.2.cloned.1.call-start = ((), (), s32[]{:S(2)}) async-start(), calls=%async_computation.1 | async-start | bytes 393216 | tf_op jit(solution)/shard_map/reduce_scatter | solution.py:55
  12.3 18.2 %copy-start.5 = (f32[24]{0:T(128)}, f32[24]{0:T(128)S(1)}, u32[]{:S(2)}) copy-start(f32[24]{0:T(128)S(1)} %compare_convert_fusion) | copy-start | bytes 292
  28.2 2.3 %copy-start = (f32[24,64,128]{2,1,0:T(8,128)S(1)}, f32[24,64,128]{2,1,0:T(8,128)}, u32[]{:S(2)}) copy-start(f32[24,64,128]{2,1,0:T(8,128)} %param.14) | copy-start | bytes 2359300
  28.3 3.7 %copy-start.7 = (s32[24]{0:T(128)S(1)}, s32[24]{0:T(128)}, u32[]{:S(2)}) copy-start(s32[24]{0:T(128)} %param.16) | copy-start | bytes 292
  31.9 6.7 %copy-start.2 = (s32[2,4096]{1,0:T(2,128)S(1)}, s32[2,4096]{1,0:T(2,128)}, u32[]{:S(2)}) copy-start(s32[2,4096]{1,0:T(2,128)} %param.19) | copy-start | bytes 98308
  32.6 7.3 %copy-start.1 = (f32[8,4096]{1,0:T(8,128)S(1)}, f32[8,4096]{1,0:T(8,128)}, u32[]{:S(2)}) copy-start(f32[8,4096]{1,0:T(8,128)} %param.13) | copy-start | bytes 393220
  34.0 57.7 %collective-permute-start = (f32[16,4096]{1,0:T(8,128)}, f32[16,4096]{1,0:T(8,128)}, u32[]{:S(2)}, u32[]{:S(2)}) collective-permute-start(f32[16,4096]{1,0:T(8,128)} %slice.59), channel_id=1, source_target_pairs={{0,2},{2,4},{4,6},{6,8},{8,10},{10,12},{12,14},{14,16},{16,18},{18... | collective-permute-start | bytes 786440 | tf_op jit(solution)/shard_map/ppermute | solution.py:15
  40.5 29.7 %copy-start.3 = (pred[4096]{0:T(1024)(128)(4,1)S(1)}, pred[4096]{0:T(1024)(128)(4,1)}, u32[]{:S(2)}) copy-start(pred[4096]{0:T(1024)(128)(4,1)} %get-tuple-element.16) | copy-start | bytes 12292
  40.5 29.7 %copy-start.4 = (pred[4096]{0:T(1024)(128)(4,1)S(1)}, pred[4096]{0:T(1024)(128)(4,1)}, u32[]{:S(2)}) copy-start(pred[4096]{0:T(1024)(128)(4,1)} %get-tuple-element.17) | copy-start | bytes 12292
  90.4 15.0 %collective-permute-start.1 = (f32[2,16,4096]{2,1,0:T(8,128)S(1)}, f32[2,16,4096]{2,1,0:T(8,128)S(1)}, u32[]{:S(2)}, u32[]{:S(2)}) collective-permute-start(f32[2,16,4096]{2,1,0:T(8,128)S(1)} %get-tuple-element.6), channel_id=1, source_target_pairs={{2,0},{4,2},{6,4},{8,6},{10,8},{12,10},{14,12},{16,14},{18,16},{20... | collective-permute-start | bytes 1572872 | tf_op jit(solution)/shard_map/ppermute | solution.py:15
  108.5 2.3 %copy-start.6 = (f32[24]{0:T(128)S(1)}, f32[24]{0:T(128)}, u32[]{:S(2)}) copy-start(f32[24]{0:T(128)} %copy-done.5) | copy-start | bytes 292
  108.5 2.3 %copy-start.8 = (s32[24]{0:T(128)S(1)}, s32[24]{0:T(128)}, u32[]{:S(2)}) copy-start(s32[24]{0:T(128)} %param.15) | copy-start | bytes 292
Sparse Core Ops, SparseCore 0:
  93.5 21.5 reduce-scatter.1
where the time goes:
time: 123 us; the launch traced here: 122 us
  local copies, waits for them, and re-layouts  56.9 us (46%)
  other arithmetic  15.1 us (12%)
  waiting for transfers between devices  15.1 us (12%)
  between operations  15 us (12%)
  blocking collectives  9.67 us (8%)
  starting transfers between devices  5.98 us (5%)
  matrix products  4.18 us (3%)
    gather x2, local copies, waits for them, and re-layouts, curve_slope(): behind = jnp.take(field, adjacency[0], axis=1)  23.1 us
    gather x2, local copies, waits for them, and re-layouts, curve_slope(): ahead = jnp.take(field, adjacency[1], axis=1)  19.6 us
    ppermute x2, waiting for transfers between devices, from_behind(): return lax.ppermute(array, axis, pairs)  12 us
    all_gather x1, blocking collectives, per_device(): gathered = lax.all_gather(paired, 'grp', axis=1, tiled=True)  9.67 us
    another operation x2, other arithmetic, per_device(): paired = jnp.stack([atm_field, atm_slope])  7.37 us
    ppermute x2, starting transfers between devices, from_behind(): return lax.ppermute(array, axis, pairs)  5.94 us
    reduce_scatter x1, waiting for transfers between devices, per_device(): lax.psum_scatter(own_part, 'grp', scatter_dimension=0, tiled=True)  3.1 us
    sub x1, other arithmetic, curve_slope(): return ahead - behind  2.85 us
  transfers between devices with their start and end apart: 3, of which 2 were waited for; matrix products, arithmetic and copies ran while one was open for 41% of the time, Pallas kernels for 0%

commit v1 on v0

v1 whole, which is shorter than its diff:
```python
import functools

import jax
import jax.numpy as jnp
from jax import lax
from jax.experimental import pallas as pl
from jax.experimental.pallas import tpu as pltpu
from jax.sharding import PartitionSpec as P

TB = 64
LANES = 128
MESH = pl.DeviceIdType.MESH
F32 = jnp.float32
BF16 = jnp.bfloat16


def roll_half(x):
    return pltpu.roll(x, TB, x.ndim - 1)


def pick_lanes(load, count, index):
    low = index & (LANES - 1)
    high = index >> 7
    bits = [(high >> b) & 1 == 1 for b in range((count - 1).bit_length())]

    def tree(first, level):
        if level < 0:
            return jnp.take_along_axis(load(first), low, axis=1, mode="promise_in_bounds")
        left = tree(first, level - 1)
        right = tree(first + (1 << level), level - 1)
        return jnp.where(bits[level], right, left)

    return tree(0, len(bits) - 1)


def field_and_slope(load, count, ahead, behind, here, odd):
    rows = here.shape[0]
    half = (lax.broadcasted_iota(jnp.int32, (rows, LANES), 1) >= TB).astype(jnp.int32)
    own = half == odd
    ahead = jnp.broadcast_to(ahead, (rows, LANES))
    behind = jnp.broadcast_to(behind, (rows, LANES))
    index = jnp.where(own, ahead, roll_half(behind))
    got = pick_lanes(load, count, index)
    mixed = jnp.where(own, here, roll_half(got) - got)
    return jnp.where(half * 0 + odd == 0, mixed, roll_half(mixed))


def split(x):
    high = x.astype(BF16)
    return high, (x - high.astype(F32)).astype(BF16)


def both_halves(product):
    rows = product.shape[0] // 2
    added = product[:rows] + product[rows:]
    return added + roll_half(added)


def kernel(
    n_sfc,
    ocean_hbm,
    atm_hbm,
    weights_hbm,
    source_hbm,
    target_hbm,
    count_hbm,
    ocean_adj_hbm,
    atm_adj_hbm,
    atm_out,
    ocean_out,
    ocean,
    fields,
    ocean_adj,
    atm_adj,
    weights,
    source,
    target,
    count,
    picked,
    terms,
    partial,
    from_partner,
    from_behind,
    ocean_tiles,
    ocean_links,
    field_tiles,
    atm_links,
    local_sem,
    send_sem,
    recv_sem,
):
    s = lax.axis_index("sfc")
    g = lax.axis_index("grp")
    columns, ocean_cells = ocean.shape
    half_columns, atm_cells = atm_hbm.shape
    tiles = weights.shape[0]
    half_cells = atm_cells // 2
    following = lax.rem(s + 1, n_sfc)
    before = lax.rem(s + n_sfc - 1, n_sfc)

    def local(src, dst, number):
        copy = pltpu.make_async_copy(src, dst, local_sem.at[number])
        copy.start()
        return copy

    def remote(src, dst, number, sfc, grp):
        return pltpu.make_async_remote_copy(
            src_ref=src,
            dst_ref=dst,
            send_sem=send_sem.at[number],
            recv_sem=recv_sem.at[number],
            device_id={"sfc": sfc, "grp": grp},
            device_id_type=MESH,
        )

    barrier = pltpu.get_barrier_semaphore()

    def greet(sfc, grp):
        pl.semaphore_signal(
            barrier, inc=1, device_id={"sfc": sfc, "grp": grp}, device_id_type=MESH
        )

    greet(s, 1 - g)
    greet(before, 1)

    @pl.when(g == 1)
    def _():
        greet(following, 0)
        greet(following, 1)

    small = [
        local(source_hbm, source, 0),
        local(target_hbm, target, 1),
        local(count_hbm, count, 2),
        local(ocean_adj_hbm, ocean_adj, 3),
        local(ocean_hbm, ocean, 4),
    ]
    weights_copy = local(weights_hbm, weights, 5)
    later = [
        local(atm_hbm, fields.at[0, pl.ds(pl.multiple_of(half_columns * g, 8), half_columns)], 6),
        local(atm_adj_hbm, atm_adj.at[0], 7),
    ]

    @pl.when(g == 0)
    def _():
        pl.semaphore_wait(barrier, 2)

    @pl.when(g == 1)
    def _():
        pl.semaphore_wait(barrier, 4)

    def partner_field(part):
        return remote(
            atm_hbm, fields.at[0, half_columns * part : half_columns * (part + 1)], 0, s, 1 - part
        )

    def before_field(part):
        return remote(
            atm_hbm,
            fields.at[1, half_columns * part : half_columns * (part + 1)],
            1 + part,
            before,
            1,
        )

    def before_adjacency():
        cells = pl.ds(0, half_cells)
        return remote(atm_adj_hbm.at[:, cells], atm_adj.at[1, :, cells], 3, before, 1)

    @pl.when(g == 0)
    def _():
        before_adjacency().start()
        before_field(0).start()
        partner_field(0).start()

    @pl.when(g == 1)
    def _():
        before_field(1).start()
        partner_field(1).start()

    for copy in small:
        copy.wait()

    live = count[0]
    for k in range(ocean_cells // LANES):
        ocean_tiles[k] = ocean[:, k * LANES : (k + 1) * LANES]
        ocean_links[k] = ocean_adj[:, k * LANES : (k + 1) * LANES]

    def pick_ocean(t, carry):
        block = source[t]
        cells = block >> 1
        x = field_and_slope(
            lambda k: ocean[:, k * LANES : (k + 1) * LANES],
            ocean_cells // LANES,
            ocean_links[cells, 1:2],
            ocean_links[cells, 0:1],
            ocean_tiles[cells],
            block & 1,
        )
        high, low = split(x)
        picked[t, :columns] = high
        picked[t, columns:] = low
        return carry

    lax.fori_loop(0, tiles, pick_ocean, 0)
    weights_copy.wait()

    def forward(t, carry):
        high, low = split(weights[t])
        both = jnp.concatenate([high, low], axis=0)
        product = lax.dot_general(
            picked[t], both, (((1,), (1,)), ((), ())), preferred_element_type=F32
        )
        terms[t] = both_halves(product)
        return carry

    def each_tile(body, group):
        def step(i, carry):
            for j in range(group):
                body(i * group + j, carry)
            return carry

        lax.fori_loop(0, tiles // group, step, 0)

    each_tile(forward, 4)

    half = (lax.broadcasted_iota(jnp.int32, (columns, LANES), 1) >= TB).astype(jnp.int32)

    def gathered_sum(p, blocks):
        here = half + 2 * p
        total = jnp.zeros((columns, LANES), F32)
        for t in range(tiles):
            total = total + jnp.where(here == blocks[t], terms[t], 0.0)
        return total

    run_start = g * (half_cells // TB)
    target_run = [
        jnp.where(t < live, target[t] - run_start, -1) for t in range(tiles)
    ]

    def add_targets(p, carry):
        cells = pl.ds(pl.multiple_of(p * LANES, LANES), LANES)
        partial[:, cells] = gathered_sum(p, target_run)
        return carry

    low_cells, high_cells = pl.ds(0, half_cells), pl.ds(half_cells, half_cells)
    low_columns, high_columns = pl.ds(0, half_columns), pl.ds(half_columns, half_columns)
    mid = half_cells // LANES

    def following_sum(part):
        return remote(
            partial.at[pl.ds(half_columns * part, half_columns), high_cells],
            from_behind,
            5 + part,
            following,
            part,
        )

    def partner_sum(part):
        if part == 0:
            return remote(partial.at[high_columns], from_partner, 4, s, 1)
        return remote(
            partial.at[low_columns, low_cells], from_partner.at[:, low_cells], 4, s, 0
        )

    lax.fori_loop(mid, 2 * mid, add_targets, 0)

    @pl.when(g == 1)
    def _():
        following_sum(0).start()
        following_sum(1).start()

    lax.fori_loop(0, mid, add_targets, 0)

    @pl.when(g == 0)
    def _():
        partner_sum(0).start()

    @pl.when(g == 1)
    def _():
        partner_sum(1).start()

    for copy in later:
        copy.wait()

    @pl.when(g == 0)
    def _():
        partner_field(1).wait_recv()

    @pl.when(g == 1)
    def _():
        partner_field(0).wait_recv()
        before_field(0).wait_recv()
        before_field(1).wait_recv()
        before_adjacency().wait_recv()

    atm_tiles = atm_cells // LANES
    for k in range(2 * atm_tiles):
        lanes = pl.ds(k % atm_tiles * LANES, LANES)
        field_tiles[k] = fields[k // atm_tiles, :, lanes]
        atm_links[k] = atm_adj[k // atm_tiles, :, lanes]

    atm_blocks = atm_cells // TB
    last_block = atm_blocks - 1 + g * (atm_blocks // 2)
    is_last = s == n_sfc - 1

    def pick_atm(t, carry):
        window_block = jnp.minimum(target[t], last_block)
        past = (window_block >= atm_blocks).astype(jnp.int32)
        block = window_block - past * atm_blocks
        cells = block >> 1
        x = field_and_slope(
            lambda k: field_tiles[past * (atm_cells // LANES) + k],
            atm_cells // LANES,
            atm_links[past * (atm_cells // LANES) + cells, 1:2],
            atm_links[past * (atm_cells // LANES) + cells, 0:1],
            field_tiles[past * (atm_cells // LANES) + cells],
            block & 1,
        )
        x = jnp.where(half * 0 + past * is_last.astype(jnp.int32) == 0, x, 0.0)
        high, low = split(x)
        picked[t, :columns] = high
        picked[t, columns:] = low
        return carry

    lax.fori_loop(0, tiles, pick_atm, 0)

    def backward(t, carry):
        weight = weights[t]
        lower = lax.broadcasted_iota(jnp.int32, weight.shape, 1) < TB
        high = weight.astype(BF16).astype(F32)
        low = weight - high
        turned = roll_half(jnp.where(lower, low, high))
        both = jnp.concatenate(
            [jnp.where(lower, high, turned), jnp.where(lower, turned, low)], axis=0
        ).astype(BF16)
        terms[t] = both_halves(jnp.dot(picked[t], both, preferred_element_type=F32))
        return carry

    each_tile(backward, 4)
    source_run = [jnp.where(t < live, source[t], -1) for t in range(tiles)]

    def add_sources(p, carry):
        cells = pl.ds(pl.multiple_of(p * LANES, LANES), LANES)
        ocean_out[:, cells] = gathered_sum(p, source_run)
        return carry

    lax.fori_loop(0, ocean_cells // LANES, add_sources, 0)

    @pl.when(g == 0)
    def _():
        partner_sum(1).wait_recv()
        following_sum(0).wait_recv()
        behind = jnp.where(s == 0, 0.0, from_behind[...])
        atm_out[:, low_cells] = partial[low_columns, low_cells] + behind
        atm_out[:, high_cells] = partial[low_columns, high_cells] + from_partner[:, low_cells]

    @pl.when(g == 1)
    def _():
        partner_sum(0).wait_recv()
        following_sum(1).wait_recv()
        behind = jnp.where(s == 0, 0.0, from_behind[...])
        atm_out[:, low_cells] = from_partner[:, low_cells] + behind
        atm_out[:, high_cells] = from_partner[:, high_cells] + partial[high_columns, low_cells]

    @pl.when(g == 0)
    def _():
        before_adjacency().wait_send()
        before_field(0).wait_send()
        partner_field(0).wait_send()
        partner_sum(0).wait_send()

    @pl.when(g == 1)
    def _():
        before_field(1).wait_send()
        partner_field(1).wait_send()
        partner_sum(1).wait_send()
        following_sum(0).wait_send()
        following_sum(1).wait_send()


def per_device(
    n_sfc,
    ocean_field,
    atm_field,
    tile_weights,
    tile_source,
    tile_target,
    tile_count,
    ocean_adjacency,
    atm_adjacency,
):
    columns, ocean_cells = ocean_field.shape
    half_columns, atm_cells = atm_field.shape
    tiles = tile_source.shape[0]
    return pl.pallas_call(
        functools.partial(kernel, n_sfc),
        out_shape=(
            jax.ShapeDtypeStruct((half_columns, atm_cells), F32),
            jax.ShapeDtypeStruct((columns, ocean_cells), F32),
        ),
        in_specs=[pl.BlockSpec(memory_space=pltpu.HBM)] * 8,
        out_specs=(
            pl.BlockSpec(memory_space=pltpu.VMEM),
            pl.BlockSpec(memory_space=pltpu.VMEM),
        ),
        scratch_shapes=[
            pltpu.VMEM((columns, ocean_cells), F32),
            pltpu.VMEM((2, columns, atm_cells), F32),
            pltpu.VMEM((2, ocean_cells), jnp.int32),
            pltpu.VMEM((2, 2, atm_cells), jnp.int32),
            pltpu.VMEM(tile_weights.shape, F32),
            pltpu.SMEM((tiles,), jnp.int32),
            pltpu.SMEM((tiles,), jnp.int32),
            pltpu.SMEM((1,), jnp.int32),
            pltpu.VMEM((tiles, 2 * columns, LANES), BF16),
            pltpu.VMEM((tiles, columns, LANES), F32),
            pltpu.VMEM((columns, atm_cells), F32),
            pltpu.VMEM((half_columns, atm_cells), F32),
            pltpu.VMEM((half_columns, atm_cells // 2), F32),
            pltpu.VMEM((ocean_cells // LANES, columns, LANES), F32),
            pltpu.VMEM((ocean_cells // LANES, 2, LANES), jnp.int32),
            pltpu.VMEM((2 * atm_cells // LANES, columns, LANES), F32),
            pltpu.VMEM((2 * atm_cells // LANES, 2, LANES), jnp.int32),
            pltpu.SemaphoreType.DMA((8,)),
            pltpu.SemaphoreType.DMA((7,)),
            pltpu.SemaphoreType.DMA((7,)),
        ],
        compiler_params=pltpu.CompilerParams(
            collective_id=0, has_side_effects=True, vmem_limit_bytes=63 * 1024 * 1024
        ),
    )(
        ocean_field,
        atm_field,
        tile_weights,
        tile_source,
        tile_target,
        tile_count,
        ocean_adjacency,
        atm_adjacency,
    )


def solution(mesh):
    return jax.shard_map(
        functools.partial(per_device, mesh.shape["sfc"]),
        mesh=mesh,
        in_specs=(
            P(None, ("sfc", "grp")),
            P("grp", "sfc"),
            P(("sfc", "grp"), None, None),
            P(("sfc", "grp")),
            P(("sfc", "grp")),
            P(("sfc", "grp")),
            P(None, ("sfc", "grp")),
            P(None, "sfc"),
        ),
        out_specs=(P("grp", "sfc"), P(None, ("sfc", "grp"))),
        check_vma=False,
    )
```

time: 123 us -> 44.9 us (0.37)
  local copies, waits for them, and re-layouts: 56.9 us -> 2.26 us
  Pallas kernels: 0 us -> 41.2 us
  other arithmetic: 15.1 us -> 0 us
  waiting for transfers between devices: 15.1 us -> 0 us
  between operations: 15 us -> 1.29 us
  blocking collectives: 9.67 us -> 0 us
  starting transfers between devices: 5.98 us -> 0 us
  matrix products: 4.18 us -> 0 us
    gather x8 -> x0, local copies, waits for them, and re-layouts: 45.3 us -> none  [the longest x2 23.1 us: curve_slope(): behind = jnp.take(field, adjacency[0], axis=1)]
    pallas_call x0 -> x1, Pallas kernels: none -> 41.2 us  [per_device(): pl.pallas_call(functools.partial(kernel, n_sfc), out_shape=(jax.ShapeDtyp...]
    ppermute x2 -> x0, waiting for transfers between devices: 12 us -> none  [from_behind(): return lax.ppermute(array, axis, pairs)]
    all_gather x1 -> x0, blocking collectives: 9.67 us -> none  [per_device(): gathered = lax.all_gather(paired, 'grp', axis=1, tiled=True)]
    another operation x2 -> x0, other arithmetic: 7.37 us -> none  [per_device(): paired = jnp.stack([atm_field, atm_slope])]
    ppermute x2 -> x0, starting transfers between devices: 5.94 us -> none  [from_behind(): return lax.ppermute(array, axis, pairs)]
    dot_general x5 -> x0, matrix products: 4.18 us -> none  [the longest x1 1.39 us: per_device(): jnp.einsum('tik,ctk->cti', tile_weights, joined, precision=HIGH)]
    reduce_scatter x1 -> x0, waiting for transfers between devices: 3.1 us -> none  [per_device(): lax.psum_scatter(own_part, 'grp', scatter_dimension=0, tiled=True)]
  transfers between devices with their start and end apart: 3 -> 0, of which waited for: 2 -> 0; matrix products, arithmetic and copies ran while one was open for 41% -> 0% of each run, Pallas kernels for 0% -> 0%
where the time goes in v1:
time: 44.9 us; the launch traced here: 44.7 us
  Pallas kernels  41.2 us (92%)
  local copies, waits for them, and re-layouts  2.26 us (5%)
  between operations  1.29 us (3%)
    pallas_call x1, Pallas kernels, per_device(): pl.pallas_call(functools.partial(kernel, n_sfc), out_shape=(jax.ShapeDtyp...  41.2 us
    unnamed x4, local copies, waits for them, and re-layouts  2.26 us

profile of v1, /device:TPU:1, one launch (start us, length us, event | category | flops | bytes accessed | tf_op | source)
XLA Modules:
  0.0 44.7 jit_solution(10524149183137454567)
XLA Ops:
  1.3 41.2 %shard_map.95 = (f32[8,4096]{1,0:T(8,128)}, f32[16,2048]{1,0:T(8,128)}) custom-call(f32[16,2048]{1,0:T(8,128)} %ocean_hbm.1, f32[8,4096]{1,0:T(8,128)} %atm_hbm.1, f32[24,64,128]{2,1,0:T(8,128)} %weights_hbm.1, s32[24]{0:T(128)} %source_hbm.1, s32[24]{0:T(128)} %target_hbm.1, s32[1]{0:T(128)S(6)} %copy.12.count_hbm, s32[2,2048]{1,0:T(2,128)} %ocean_adj_hbm.1, ...), custom_call_target="tpu_custom_call" | custom-call | tf_op jit(solution)/shard_map/pallas_call | solution.py:396
  42.4 0.0 copy-start
  42.5 1.6 %copy.13 = f32[8,4096]{1,0:T(8,128)} copy(f32[8,4096]{1,0:T(8,128)} %get-tuple-element.4) | data formatting | bytes 262144
  44.1 0.0 copy-done
  44.1 0.7 %copy.14 = f32[16,2048]{1,0:T(8,128)} copy(f32[16,2048]{1,0:T(8,128)S(1)} %copy-done) | data formatting | bytes 262144
Async XLA Ops:
  42.4 1.6 %copy-start = (f32[16,2048]{1,0:T(8,128)S(1)}, f32[16,2048]{1,0:T(8,128)}, u32[]{:S(2)}) copy-start(f32[16,2048]{1,0:T(8,128)} %get-tuple-element.5) | copy-start | bytes 393220

commit v2 on v0

v2 whole, which is shorter than its diff:
```python
import functools

import jax
import jax.numpy as jnp
from jax import lax
from jax.experimental import pallas as pl
from jax.experimental.pallas import tpu as pltpu
from jax.sharding import PartitionSpec as P

TB = 64
LANES = 128
ROWS = 8
GATHER = 24
JOIN = 24
VLIM = 63 * 1024 * 1024
MESH = pl.DeviceIdType.MESH
F32 = jnp.float32
BF16 = jnp.bfloat16


def roll_half(x):
    return pltpu.roll(x, TB, x.ndim - 1)


def lower_lanes(rows):
    return lax.broadcasted_iota(jnp.int32, (rows, LANES), 1) < TB


def pick_lanes(load, count, index):
    low = index & (LANES - 1)
    high = index >> 7
    bits = [(high >> b) & 1 == 1 for b in range((count - 1).bit_length())]

    def tree(first, level):
        if level < 0:
            return jnp.take_along_axis(load(first), low, axis=1, mode="promise_in_bounds")
        left = tree(first, level - 1)
        right = tree(first + (1 << level), level - 1)
        return jnp.where(bits[level], right, left)

    return tree(0, len(bits) - 1)


def stacked(x):
    high = x.astype(BF16).astype(F32)
    return jnp.concatenate([high, x - high], axis=0).astype(BF16)


def block_links(links):
    ahead = jnp.broadcast_to(links[1:2], (ROWS, LANES))
    behind = jnp.broadcast_to(links[0:1], (ROWS, LANES))
    lower = lower_lanes(ROWS)
    return (
        jnp.where(lower, ahead, roll_half(behind)),
        jnp.where(lower, roll_half(ahead), behind),
    )


def each(count, group, body):
    def step(i, carry):
        for j in range(group):
            body(i * group + j)
        return carry

    if group == count:
        step(0, 0)
    else:
        lax.fori_loop(0, count // group, step, 0)


def kernel(
    n_sfc,
    ocean_hbm,
    atm_hbm,
    weights_hbm,
    source_hbm,
    target_hbm,
    count_hbm,
    ocean_adj_hbm,
    atm_adj_hbm,
    atm_out,
    ocean_out,
    ocean,
    own_fields,
    partner_fields,
    ocean_adj,
    atm_adj,
    weights,
    source,
    target,
    count,
    ocean_links,
    atm_links,
    split_weights,
    got,
    picked,
    terms,
    places,
    partial,
    from_partner,
    from_behind,
    local_sem,
    send_sem,
    recv_sem,
):
    s = lax.axis_index("sfc")
    g = lax.axis_index("grp")
    ocean_tiles = ocean.shape[1]
    atm_tiles = atm_hbm.shape[0]
    half_tiles = atm_tiles // 2
    tiles = weights.shape[0]
    has_following = s < n_sfc - 1
    has_before = s > 0
    following = jnp.minimum(s + 1, n_sfc - 1)
    before = jnp.maximum(s - 1, 0)
    sends_on = jnp.logical_and(g == 1, has_following)

    def local(src, dst, number):
        return pltpu.make_async_copy(src, dst, local_sem.at[number])

    def remote(src, dst, number, sfc, grp):
        return pltpu.make_async_remote_copy(
            src_ref=src,
            dst_ref=dst,
            send_sem=send_sem.at[number],
            recv_sem=recv_sem.at[number],
            device_id={"sfc": sfc, "grp": grp},
            device_id_type=MESH,
        )

    barrier = pltpu.get_barrier_semaphore()

    def greet(sfc, grp):
        pl.semaphore_signal(
            barrier, inc=1, device_id={"sfc": sfc, "grp": grp}, device_id_type=MESH
        )

    greet(s, 1 - g)

    @pl.when(has_before)
    def _():
        greet(before, 1)

    @pl.when(sends_on)
    def _():
        greet(following, 0)
        greet(following, 1)

    small_copies = [
        local(source_hbm, source, 0),
        local(target_hbm, target, 1),
        local(count_hbm, count, 2),
        local(ocean_adj_hbm, ocean_adj, 3),
        local(ocean_hbm, ocean, 4),
    ]
    weights_copy = local(weights_hbm, weights, 5)
    field_copy = local(atm_hbm, own_fields.at[0], 6)
    low_adj_copy = local(atm_adj_hbm.at[pl.ds(g * half_tiles, half_tiles)], atm_adj.at[0], 7)
    high_adj_copy = local(atm_adj_hbm.at[pl.ds(half_tiles, half_tiles)], atm_adj.at[1], 8)
    for copy in small_copies + [weights_copy, field_copy, low_adj_copy]:
        copy.start()

    @pl.when(g == 0)
    def _():
        high_adj_copy.start()

    peers = 1 + has_before.astype(jnp.int32) + 2 * sends_on.astype(jnp.int32)
    pl.semaphore_wait(barrier, peers)

    def partner_field(part):
        return remote(atm_hbm, partner_fields.at[0], 0, s, 1 - part)

    def before_field(part):
        landing = own_fields if part == 1 else partner_fields
        return remote(atm_hbm, landing.at[1], 1 + part, before, 1)

    def before_adjacency():
        return remote(atm_adj_hbm.at[pl.ds(0, half_tiles)], atm_adj.at[1], 3, before, 1)

    @pl.when(g == 0)
    def _():
        partner_field(0).start()

        @pl.when(has_before)
        def _():
            before_adjacency().start()
            before_field(0).start()

    @pl.when(g == 1)
    def _():
        partner_field(1).start()

        @pl.when(has_before)
        def _():
            before_field(1).start()

    for copy in small_copies:
        copy.wait()

    live = count[0]
    upper = 1 - lower_lanes(ROWS).astype(jnp.int32)

    def store_links(links, first, adjacency, number):
        for k in range(number):
            even, odd = block_links(adjacency[k])
            links[first + 2 * k] = even
            links[first + 2 * k + 1] = odd

    def store_places(block_of):
        for t in range(tiles):
            places[t] = jnp.where(t < live, block_of(t), -2) - upper

    def scatter(out, part, number):
        group = 4

        def step(i, carry):
            sums = [jnp.zeros((ROWS, LANES), F32) for _ in range(group)]
            for t in range(tiles):
                place, term = places[t], terms[t]
                for j in range(group):
                    first = 2 * (i * group + j)
                    sums[j] = sums[j] + jnp.where(place == first, term, 0.0)
            for j in range(group):
                out[part, i * group + j] = sums[j]
            return carry

        lax.fori_loop(0, number // group, step, 0)

    def pick_ocean(part):
        def gather(t):
            got[t] = pick_lanes(lambda k: ocean[part, k], ocean_tiles, ocean_links[source[t]])

        each(tiles, GATHER, gather)

        def join(t):
            block = source[t]
            tile = ocean[part, block >> 1]
            field = jnp.where(upper * 0 + (block & 1) == 0, tile, roll_half(tile))
            slope = roll_half(got[t]) - got[t]
            picked[t, : 2 * ROWS] = stacked(jnp.where(lower_lanes(ROWS), field, slope))

        each(tiles, JOIN, join)

    def forward():
        for t in range(tiles):
            product = lax.dot_general(
                picked[t, : 2 * ROWS],
                split_weights[t],
                (((1,), (1,)), ((), ())),
                preferred_element_type=F32,
            )
            added = product[:ROWS] + product[ROWS:]
            terms[t] = added + roll_half(added)

    run_start = g * half_tiles * 2
    store_links(ocean_links, 0, ocean_adj, ocean_tiles)
    store_places(lambda t: target[t] - run_start)
    pick_ocean(1 - g)
    weights_copy.wait()

    def split(t):
        split_weights[t] = stacked(weights[t])

    each(tiles, 4, split)
    forward()
    scatter(partial, 0, atm_tiles)

    low_half, high_half = pl.ds(0, half_tiles), pl.ds(half_tiles, half_tiles)

    def following_sum(part):
        return remote(partial.at[part, high_half], from_behind, 5 + part, following, part)

    def partner_sum(part):
        if part == 0:
            return remote(partial.at[0], from_partner, 4, s, 1)
        return remote(partial.at[0, low_half], from_partner.at[low_half], 4, s, 0)

    @pl.when(g == 0)
    def _():
        partner_sum(0).start()

    @pl.when(g == 1)
    def _():
        partner_sum(1).start()

    @pl.when(sends_on)
    def _():
        following_sum(0).start()

    pick_ocean(g)
    forward()
    scatter(partial, 1, atm_tiles)

    @pl.when(sends_on)
    def _():
        following_sum(1).start()

    is_last = jnp.logical_not(has_following).astype(jnp.int32)

    def pick_atm(fields):
        def place_of(t):
            block = jnp.clip(target[t] - run_start, 0, 2 * atm_tiles - 1)
            past = g * (block >= atm_tiles).astype(jnp.int32)
            return block, past

        def gather(t):
            block, past = place_of(t)
            got[t] = pick_lanes(
                lambda k: fields[past, k], atm_tiles, atm_links[block]
            )

        each(tiles, GATHER, gather)

        def join(t):
            block, past = place_of(t)
            tile = fields[past, (block + run_start - 2 * atm_tiles * past) >> 1]
            turned = roll_half(tile)
            lower = lower_lanes(ROWS)
            keep = upper * 0 + past * is_last == 0
            field = jnp.where(upper == (block & 1), tile, turned)
            ahead = roll_half(got[t]) - got[t]
            slope = jnp.where(lower, -ahead, ahead)
            picked[t, : 2 * ROWS] = stacked(jnp.where(keep, field, 0.0))
            picked[t, 2 * ROWS :] = stacked(jnp.where(keep, slope, 0.0))

        each(tiles, JOIN, join)

    def backward():
        lower = lower_lanes(ROWS)
        for t in range(tiles):
            product = jnp.dot(picked[t], split_weights[t], preferred_element_type=F32)
            field = product[:ROWS] + product[ROWS : 2 * ROWS]
            slope = product[2 * ROWS : 3 * ROWS] + product[3 * ROWS :]
            both = jnp.where(lower, field, slope)
            terms[t] = both + roll_half(both)

    low_adj_copy.wait()
    field_copy.wait()

    @pl.when(g == 0)
    def _():
        high_adj_copy.wait()

    @pl.when(sends_on)
    def _():
        before_adjacency().wait_recv()
        before_field(1).wait_recv()

    store_links(atm_links, 0, atm_adj.at[0], half_tiles)
    store_links(atm_links, 2 * half_tiles, atm_adj.at[1], half_tiles)
    store_places(lambda t: source[t])
    pick_atm(own_fields)
    backward()
    scatter(ocean_out, g, ocean_tiles)

    @pl.when(g == 0)
    def _():
        partner_field(1).wait_recv()

    @pl.when(g == 1)
    def _():
        partner_field(0).wait_recv()

    @pl.when(sends_on)
    def _():
        before_field(0).wait_recv()

    pick_atm(partner_fields)
    backward()
    scatter(ocean_out, 1 - g, ocean_tiles)

    def behind_sum():
        return jnp.where(has_before, from_behind[...], 0.0)

    @pl.when(g == 0)
    def _():
        partner_sum(1).wait_recv()

        @pl.when(has_before)
        def _():
            following_sum(0).wait_recv()

        atm_out[low_half] = partial[1, low_half] + behind_sum()
        atm_out[high_half] = partial[1, high_half] + from_partner[low_half]

    @pl.when(g == 1)
    def _():
        partner_sum(0).wait_recv()

        @pl.when(has_before)
        def _():
            following_sum(1).wait_recv()

        atm_out[low_half] = from_partner[low_half] + behind_sum()
        atm_out[high_half] = from_partner[high_half] + partial[1, low_half]

    @pl.when(g == 0)
    def _():
        partner_field(0).wait_send()
        partner_sum(0).wait_send()

        @pl.when(has_before)
        def _():
            before_adjacency().wait_send()
            before_field(0).wait_send()

    @pl.when(g == 1)
    def _():
        partner_field(1).wait_send()
        partner_sum(1).wait_send()

        @pl.when(has_before)
        def _():
            before_field(1).wait_send()

    @pl.when(sends_on)
    def _():
        following_sum(0).wait_send()
        following_sum(1).wait_send()


def as_tiles(x):
    rows, cells = x.shape
    return x.reshape(rows, cells // LANES, LANES).transpose(1, 0, 2)


def write_kernel(atm, ocean, atm_out, ocean_out, sem):
    copies = [
        pltpu.make_async_copy(atm, atm_out, sem.at[0]),
        pltpu.make_async_copy(ocean, ocean_out, sem.at[1]),
    ]
    for copy in copies:
        copy.start()
    for copy in copies:
        copy.wait()


def write_out(atm, ocean):
    return pl.pallas_call(
        write_kernel,
        out_shape=(
            jax.ShapeDtypeStruct(atm.shape, F32),
            jax.ShapeDtypeStruct(ocean.shape, F32),
        ),
        in_specs=[pl.BlockSpec(memory_space=pltpu.VMEM)] * 2,
        out_specs=[pl.BlockSpec(memory_space=pltpu.HBM)] * 2,
        scratch_shapes=[pltpu.SemaphoreType.DMA((2,))],
    )(
        pltpu.with_memory_space_constraint(atm, pltpu.VMEM),
        pltpu.with_memory_space_constraint(ocean, pltpu.VMEM),
    )


def per_device(
    n_sfc,
    ocean_field,
    atm_field,
    tile_weights,
    tile_source,
    tile_target,
    tile_count,
    ocean_adjacency,
    atm_adjacency,
):
    columns, ocean_cells = ocean_field.shape
    half_columns, atm_cells = atm_field.shape
    tiles = tile_source.shape[0]
    ocean_tiles = ocean_cells // LANES
    atm_tiles = atm_cells // LANES
    half_tiles = atm_tiles // 2
    vmem = pl.BlockSpec(memory_space=pltpu.VMEM)
    atm_out, ocean_out = pl.pallas_call(
        functools.partial(kernel, n_sfc),
        out_shape=(
            pltpu.VMEM((atm_tiles, ROWS, LANES), F32),
            pltpu.VMEM((2, ocean_tiles, ROWS, LANES), F32),
        ),
        in_specs=[pl.BlockSpec(memory_space=pltpu.HBM)] * 8,
        out_specs=(vmem, vmem),
        scratch_shapes=[
            pltpu.VMEM((2, ocean_tiles, ROWS, LANES), F32),
            pltpu.VMEM((2, atm_tiles, ROWS, LANES), F32),
            pltpu.VMEM((2, atm_tiles, ROWS, LANES), F32),
            pltpu.VMEM((ocean_tiles, 2, LANES), jnp.int32),
            pltpu.VMEM((2, half_tiles, 2, LANES), jnp.int32),
            pltpu.VMEM(tile_weights.shape, F32),
            pltpu.SMEM((tiles,), jnp.int32),
            pltpu.SMEM((tiles,), jnp.int32),
            pltpu.SMEM((1,), jnp.int32),
            pltpu.VMEM((2 * ocean_tiles, ROWS, LANES), jnp.int32),
            pltpu.VMEM((2 * atm_tiles, ROWS, LANES), jnp.int32),
            pltpu.VMEM((tiles, 2 * TB, LANES), BF16),
            pltpu.VMEM((tiles, ROWS, LANES), F32),
            pltpu.VMEM((tiles, 4 * ROWS, LANES), BF16),
            pltpu.VMEM((tiles, ROWS, LANES), F32),
            pltpu.VMEM((tiles, ROWS, LANES), jnp.int32),
            pltpu.VMEM((2, atm_tiles, ROWS, LANES), F32),
            pltpu.VMEM((atm_tiles, ROWS, LANES), F32),
            pltpu.VMEM((half_tiles, ROWS, LANES), F32),
            pltpu.SemaphoreType.DMA((9,)),
            pltpu.SemaphoreType.DMA((7,)),
            pltpu.SemaphoreType.DMA((7,)),
        ],
        compiler_params=pltpu.CompilerParams(
            collective_id=0, has_side_effects=True, vmem_limit_bytes=VLIM
        ),
    )(
        ocean_field.reshape(2, ROWS, ocean_tiles, LANES).transpose(0, 2, 1, 3),
        as_tiles(atm_field),
        tile_weights,
        tile_source,
        tile_target,
        tile_count,
        as_tiles(ocean_adjacency),
        as_tiles(atm_adjacency),
    )
    atm_out, ocean_out = write_out(atm_out, ocean_out)
    return (
        atm_out.transpose(1, 0, 2).reshape(half_columns, atm_cells),
        ocean_out.transpose(0, 2, 1, 3).reshape(columns, ocean_cells),
    )


def solution(mesh):
    return jax.shard_map(
        functools.partial(per_device, mesh.shape["sfc"]),
        mesh=mesh,
        in_specs=(
            P(None, ("sfc", "grp")),
            P("grp", "sfc"),
            P(("sfc", "grp"), None, None),
            P(("sfc", "grp")),
            P(("sfc", "grp")),
            P(("sfc", "grp")),
            P(None, ("sfc", "grp")),
            P(None, "sfc"),
        ),
        out_specs=(P("grp", "sfc"), P(None, ("sfc", "grp"))),
        check_vma=False,
    )
```

time: 123 us -> 20 us (0.16)
  local copies, waits for them, and re-layouts: 56.9 us -> 0 us
  Pallas kernels: 0 us -> 18.6 us
  other arithmetic: 15.1 us -> 0 us
  waiting for transfers between devices: 15.1 us -> 0 us
  between operations: 15 us -> 1.29 us
  blocking collectives: 9.67 us -> 0 us
  starting transfers between devices: 5.98 us -> 0 us
  matrix products: 4.18 us -> 0 us
    gather x8 -> x0, local copies, waits for them, and re-layouts: 45.3 us -> none  [the longest x2 23.1 us: curve_slope(): behind = jnp.take(field, adjacency[0], axis=1)]
    pallas_call x0 -> x2, Pallas kernels: none -> 18.6 us  [the longest x1 17.8 us: per_device(): pl.pallas_call(functools.partial(kernel, n_sfc), out_shape=(pltpu.VMEM((a...]
    ppermute x2 -> x0, waiting for transfers between devices: 12 us -> none  [from_behind(): return lax.ppermute(array, axis, pairs)]
    all_gather x1 -> x0, blocking collectives: 9.67 us -> none  [per_device(): gathered = lax.all_gather(paired, 'grp', axis=1, tiled=True)]
    another operation x2 -> x0, other arithmetic: 7.37 us -> none  [per_device(): paired = jnp.stack([atm_field, atm_slope])]
    ppermute x2 -> x0, starting transfers between devices: 5.94 us -> none  [from_behind(): return lax.ppermute(array, axis, pairs)]
    dot_general x5 -> x0, matrix products: 4.18 us -> none  [the longest x1 1.39 us: per_device(): jnp.einsum('tik,ctk->cti', tile_weights, joined, precision=HIGH)]
    reduce_scatter x1 -> x0, waiting for transfers between devices: 3.1 us -> none  [per_device(): lax.psum_scatter(own_part, 'grp', scatter_dimension=0, tiled=True)]
  transfers between devices with their start and end apart: 3 -> 0, of which waited for: 2 -> 0; matrix products, arithmetic and copies ran while one was open for 41% -> 0% of each run, Pallas kernels for 0% -> 0%
where the time goes in v2:
time: 20 us; the launch traced here: 19.8 us
  Pallas kernels  18.6 us (93%)
  between operations  1.29 us (6%)
    pallas_call x1, Pallas kernels, per_device(): pl.pallas_call(functools.partial(kernel, n_sfc), out_shape=(pltpu.VMEM((a...  17.8 us
    pallas_call x1, Pallas kernels, write_out(): pl.pallas_call(write_kernel, out_shape=(jax.ShapeDtypeStruct(atm.shape, F...  0.72 us

profile of v2, /device:TPU:1, one launch (start us, length us, event | category | flops | bytes accessed | tf_op | source)
XLA Modules:
  0.0 19.8 jit_solution(15591802783087832453)
XLA Ops:
  1.3 17.8 %shard_map.95 = (f32[32,8,128]{2,1,0:T(8,128)S(1)}, f32[2,16,8,128]{3,2,1,0:T(8,128)S(1)}) custom-call(f32[2,16,8,128]{3,2,1,0:T(8,128)} %bitcast.18, f32[32,8,128]{2,1,0:T(8,128)} %bitcast.19, f32[24,64,128]{2,1,0:T(8,128)} %weights_hbm.1, s32[24]{0:T(128)} %source_hbm.1, s32[24]{0:T(128)} %target_hbm.1, s32[1]{0:T(128)S(6)} %copy.10.count_hbm, ...), custom_call_target="tpu_custom_call" | custom-call | tf_op jit(solution)/shard_map/pallas_call | solution.py:472
  19.1 0.7 %shard_map.96 = (f32[32,8,128]{2,1,0:T(8,128)}, f32[2,16,8,128]{3,2,1,0:T(8,128)}) custom-call(f32[32,8,128]{2,1,0:T(8,128)S(1)} %get-tuple-element.6.atm, f32[2,16,8,128]{3,2,1,0:T(8,128)S(1)} %get-tuple-element.7.ocean), custom_call_target="tpu_custom_call" | custom-call | tf_op jit(solution)/shard_map/pallas_call | solution.py:439

commit v3 on v2

--- a/solution.py
+++ b/solution.py
@@ -164,8 +164,12 @@
     def _():
         high_adj_copy.start()
 
-    peers = 1 + has_before.astype(jnp.int32) + 2 * sends_on.astype(jnp.int32)
-    pl.semaphore_wait(barrier, peers)
+    patient = jnp.logical_and(s == 0, g == 1)
+    prompt = jnp.logical_not(patient)
+
+    def meet():
+        peers = 1 + has_before.astype(jnp.int32) + 2 * sends_on.astype(jnp.int32)
+        pl.semaphore_wait(barrier, peers)
 
     def partner_field(part):
         return remote(atm_hbm, partner_fields.at[0], 0, s, 1 - part)
@@ -177,22 +181,27 @@
     def before_adjacency():
         return remote(atm_adj_hbm.at[pl.ds(0, half_tiles)], atm_adj.at[1], 3, before, 1)
 
-    @pl.when(g == 0)
-    def _():
-        partner_field(0).start()
-
-        @pl.when(has_before)
-        def _():
-            before_adjacency().start()
-            before_field(0).start()
-
-    @pl.when(g == 1)
-    def _():
-        partner_field(1).start()
-
-        @pl.when(has_before)
-        def _():
-            before_field(1).start()
+    def send_fields():
+        @pl.when(g == 0)
+        def _():
+            partner_field(0).start()
+
+            @pl.when(has_before)
+            def _():
+                before_adjacency().start()
+
+        @pl.when(g == 1)
+        def _():
+            partner_field(1).start()
+
+            @pl.when(has_before)
+            def _():
+                before_field(1).start()
+
+    @pl.when(prompt)
+    def _():
+        meet()
+        send_fields()
 
     for copy in small_copies:
         copy.wait()
@@ -275,25 +284,33 @@
             return remote(partial.at[0], from_partner, 4, s, 1)
         return remote(partial.at[0, low_half], from_partner.at[low_half], 4, s, 0)
 
-    @pl.when(g == 0)
-    def _():
-        partner_sum(0).start()
-
-    @pl.when(g == 1)
-    def _():
-        partner_sum(1).start()
-
-    @pl.when(sends_on)
-    def _():
-        following_sum(0).start()
-
+    def send_partner_columns():
+        @pl.when(g == 0)
+        def _():
+            partner_sum(0).start()
+
+            @pl.when(has_before)
+            def _():
+                before_field(0).start()
+
+        @pl.when(g == 1)
+        def _():
+            partner_sum(1).start()
+
+        @pl.when(sends_on)
+        def _():
+            following_sum(0).start()
+
+    def send_own_columns():
+        @pl.when(sends_on)
+        def _():
+            following_sum(1).start()
+
+    pl.when(prompt)(send_partner_columns)
     pick_ocean(g)
     forward()
     scatter(partial, 1, atm_tiles)
-
-    @pl.when(sends_on)
-    def _():
-        following_sum(1).start()
+    pl.when(prompt)(send_own_columns)
 
     is_last = jnp.logical_not(has_following).astype(jnp.int32)
 
@@ -352,6 +369,13 @@
     pick_atm(own_fields)
     backward()
     scatter(ocean_out, g, ocean_tiles)
+
+    @pl.when(patient)
+    def _():
+        meet()
+        send_fields()
+        send_partner_columns()
+        send_own_columns()
 
     @pl.when(g == 0)
     def _():

time: 20 us -> 17.3 us (0.86)
  Pallas kernels: 18.6 us -> 15.8 us
    pallas_call x1, Pallas kernels: 17.8 us -> 15.1 us  [per_device(): pl.pallas_call(functools.partial(kernel, n_sfc), out_shape=(pltpu.VMEM((a...]
where the time goes in v3:
time: 17.3 us; the launch traced here: 17.1 us
  Pallas kernels  15.8 us (91%)
  between operations  1.29 us (7%)
    pallas_call x1, Pallas kernels, per_device(): pl.pallas_call(functools.partial(kernel, n_sfc), out_shape=(pltpu.VMEM((a...  15.1 us
    pallas_call x1, Pallas kernels, write_out(): pl.pallas_call(write_kernel, out_shape=(jax.ShapeDtypeStruct(atm.shape, F...  0.72 us

profile of v3, /device:TPU:1, one launch (start us, length us, event | category | flops | bytes accessed | tf_op | source)
XLA Modules:
  0.0 17.1 jit_solution(17721587317421511071)
XLA Ops:
  1.3 15.1 %shard_map.95 = (f32[32,8,128]{2,1,0:T(8,128)S(1)}, f32[2,16,8,128]{3,2,1,0:T(8,128)S(1)}) custom-call(f32[2,16,8,128]{3,2,1,0:T(8,128)} %bitcast.18, f32[32,8,128]{2,1,0:T(8,128)} %bitcast.19, f32[24,64,128]{2,1,0:T(8,128)} %weights_hbm.1, s32[24]{0:T(128)} %source_hbm.1, s32[24]{0:T(128)} %target_hbm.1, s32[1]{0:T(128)S(6)} %copy.10.count_hbm, ...), custom_call_target="tpu_custom_call" | custom-call | tf_op jit(solution)/shard_map/pallas_call | solution.py:496
  16.4 0.7 %shard_map.96 = (f32[32,8,128]{2,1,0:T(8,128)}, f32[2,16,8,128]{3,2,1,0:T(8,128)}) custom-call(f32[32,8,128]{2,1,0:T(8,128)S(1)} %get-tuple-element.6.atm, f32[2,16,8,128]{3,2,1,0:T(8,128)S(1)} %get-tuple-element.7.ocean), custom_call_target="tpu_custom_call" | custom-call | tf_op jit(solution)/shard_map/pallas_call | solution.py:463

commit v4 on v3

--- a/solution.py
+++ b/solution.py
@@ -219,7 +219,7 @@
         for t in range(tiles):
             places[t] = jnp.where(t < live, block_of(t), -2) - upper
 
-    def scatter(out, part, number):
+    def scatter(out, part, first_tile, number):
         group = 4
 
         def step(i, carry):
@@ -227,31 +227,27 @@
             for t in range(tiles):
                 place, term = places[t], terms[t]
                 for j in range(group):
-                    first = 2 * (i * group + j)
+                    first = 2 * (first_tile + i * group + j)
                     sums[j] = sums[j] + jnp.where(place == first, term, 0.0)
             for j in range(group):
-                out[part, i * group + j] = sums[j]
+                out[part, first_tile + i * group + j] = sums[j]
             return carry
 
         lax.fori_loop(0, number // group, step, 0)
 
-    def pick_ocean(part):
-        def gather(t):
+    def pick_ocean(part, group):
+        for t in group:
             got[t] = pick_lanes(lambda k: ocean[part, k], ocean_tiles, ocean_links[source[t]])
 
-        each(tiles, GATHER, gather)
-
-        def join(t):
+        for t in group:
             block = source[t]
             tile = ocean[part, block >> 1]
             field = jnp.where(upper * 0 + (block & 1) == 0, tile, roll_half(tile))
             slope = roll_half(got[t]) - got[t]
             picked[t, : 2 * ROWS] = stacked(jnp.where(lower_lanes(ROWS), field, slope))
 
-        each(tiles, JOIN, join)
-
-    def forward():
-        for t in range(tiles):
+    def forward(group):
+        for t in group:
             product = lax.dot_general(
                 picked[t, : 2 * ROWS],
                 split_weights[t],
@@ -264,39 +260,43 @@
     run_start = g * half_tiles * 2
     store_links(ocean_links, 0, ocean_adj, ocean_tiles)
     store_places(lambda t: target[t] - run_start)
-    pick_ocean(1 - g)
     weights_copy.wait()
-
-    def split(t):
-        split_weights[t] = stacked(weights[t])
-
-    each(tiles, 4, split)
-    forward()
-    scatter(partial, 0, atm_tiles)
+    group_size = 24
+    groups = [range(i, i + group_size) for i in range(0, tiles, group_size)]
+    for group in groups:
+        pick_ocean(1 - g, group)
+        for t in group:
+            split_weights[t] = stacked(weights[t])
+        forward(group)
+    scatter(partial, 0, 0, half_tiles)
 
     low_half, high_half = pl.ds(0, half_tiles), pl.ds(half_tiles, half_tiles)
 
     def following_sum(part):
         return remote(partial.at[part, high_half], from_behind, 5 + part, following, part)
 
-    def partner_sum(part):
-        if part == 0:
-            return remote(partial.at[0], from_partner, 4, s, 1)
-        return remote(partial.at[0, low_half], from_partner.at[low_half], 4, s, 0)
-
-    def send_partner_columns():
+    def partner_low(part):
+        return remote(partial.at[0, low_half], from_partner.at[low_half], 4, s, 1 - part)
+
+    def partner_high():
+        return remote(partial.at[0, high_half], from_partner.at[high_half], 7, s, 1)
+
+    def send_low():
+        for part in range(2):
+            pl.when(g == part)(partner_low(part).start)
+
+    pl.when(prompt)(send_low)
+    scatter(partial, 0, half_tiles, half_tiles)
+
+    def send_high():
         @pl.when(g == 0)
         def _():
-            partner_sum(0).start()
+            partner_high().start()
 
             @pl.when(has_before)
             def _():
                 before_field(0).start()
 
-        @pl.when(g == 1)
-        def _():
-            partner_sum(1).start()
-
         @pl.when(sends_on)
         def _():
             following_sum(0).start()
@@ -306,10 +306,11 @@
         def _():
             following_sum(1).start()
 
-    pl.when(prompt)(send_partner_columns)
-    pick_ocean(g)
-    forward()
-    scatter(partial, 1, atm_tiles)
+    pl.when(prompt)(send_high)
+    for group in groups:
+        pick_ocean(g, group)
+        forward(group)
+    scatter(partial, 1, 0, atm_tiles)
     pl.when(prompt)(send_own_columns)
 
     is_last = jnp.logical_not(has_following).astype(jnp.int32)
@@ -368,13 +369,14 @@
     store_places(lambda t: source[t])
     pick_atm(own_fields)
     backward()
-    scatter(ocean_out, g, ocean_tiles)
+    scatter(ocean_out, g, 0, ocean_tiles)
 
     @pl.when(patient)
     def _():
         meet()
         send_fields()
-        send_partner_columns()
+        send_low()
+        send_high()
         send_own_columns()
 
     @pl.when(g == 0)
@@ -391,14 +393,14 @@
 
     pick_atm(partner_fields)
     backward()
-    scatter(ocean_out, 1 - g, ocean_tiles)
+    scatter(ocean_out, 1 - g, 0, ocean_tiles)
 
     def behind_sum():
         return jnp.where(has_before, from_behind[...], 0.0)
 
     @pl.when(g == 0)
     def _():
-        partner_sum(1).wait_recv()
+        partner_low(1).wait_recv()
 
         @pl.when(has_before)
         def _():
@@ -409,19 +411,21 @@
 
     @pl.when(g == 1)
     def _():
-        partner_sum(0).wait_recv()
+        partner_low(0).wait_recv()
 
         @pl.when(has_before)
         def _():
             following_sum(1).wait_recv()
 
         atm_out[low_half] = from_partner[low_half] + behind_sum()
+        partner_high().wait_recv()
         atm_out[high_half] = from_partner[high_half] + partial[1, low_half]
 
     @pl.when(g == 0)
     def _():
         partner_field(0).wait_send()
-        partner_sum(0).wait_send()
+        partner_low(0).wait_send()
+        partner_high().wait_send()
 
         @pl.when(has_before)
         def _():
@@ -431,7 +435,7 @@
     @pl.when(g == 1)
     def _():
         partner_field(1).wait_send()
-        partner_sum(1).wait_send()
+        partner_low(1).wait_send()
 
         @pl.when(has_before)
         def _():
@@ -522,8 +526,8 @@
             pltpu.VMEM((atm_tiles, ROWS, LANES), F32),
             pltpu.VMEM((half_tiles, ROWS, LANES), F32),
             pltpu.SemaphoreType.DMA((9,)),
-            pltpu.SemaphoreType.DMA((7,)),
-            pltpu.SemaphoreType.DMA((7,)),
+            pltpu.SemaphoreType.DMA((8,)),
+            pltpu.SemaphoreType.DMA((8,)),
         ],
         compiler_params=pltpu.CompilerParams(
             collective_id=0, has_side_effects=True, vmem_limit_bytes=VLIM

time: 17.3 us -> 17 us (0.983)
  Pallas kernels: 15.8 us -> 15.5 us
    pallas_call x1, Pallas kernels: 15.1 us -> 14.8 us  [per_device(): pl.pallas_call(functools.partial(kernel, n_sfc), out_shape=(pltpu.VMEM((a...]
where the time goes in v4:
time: 17 us; the launch traced here: 16.8 us
  Pallas kernels  15.5 us (91%)
  between operations  1.29 us (8%)
    pallas_call x1, Pallas kernels, per_device(): pl.pallas_call(functools.partial(kernel, n_sfc), out_shape=(pltpu.VMEM((a...  14.8 us
    pallas_call x1, Pallas kernels, write_out(): pl.pallas_call(write_kernel, out_shape=(jax.ShapeDtypeStruct(atm.shape, F...  0.72 us

profile of v4, /device:TPU:1, one launch (start us, length us, event | category | flops | bytes accessed | tf_op | source)
XLA Modules:
  0.0 16.8 jit_solution(1993004025458792402)
XLA Ops:
  1.3 14.8 %shard_map.95 = (f32[32,8,128]{2,1,0:T(8,128)S(1)}, f32[2,16,8,128]{3,2,1,0:T(8,128)S(1)}) custom-call(f32[2,16,8,128]{3,2,1,0:T(8,128)} %bitcast.18, f32[32,8,128]{2,1,0:T(8,128)} %bitcast.19, f32[24,64,128]{2,1,0:T(8,128)} %weights_hbm.1, s32[24]{0:T(128)} %source_hbm.1, s32[24]{0:T(128)} %target_hbm.1, s32[1]{0:T(128)S(6)} %copy.10.count_hbm, ...), custom_call_target="tpu_custom_call" | custom-call | tf_op jit(solution)/shard_map/pallas_call | solution.py:500
  16.1 0.7 %shard_map.96 = (f32[32,8,128]{2,1,0:T(8,128)}, f32[2,16,8,128]{3,2,1,0:T(8,128)}) custom-call(f32[32,8,128]{2,1,0:T(8,128)S(1)} %get-tuple-element.6.atm, f32[2,16,8,128]{3,2,1,0:T(8,128)S(1)} %get-tuple-element.7.ocean), custom_call_target="tpu_custom_call" | custom-call | tf_op jit(solution)/shard_map/pallas_call | solution.py:467

commit v5 on v4

--- a/solution.py
+++ b/solution.py
@@ -80,7 +80,8 @@
     atm_adj_hbm,
     atm_out,
     ocean_out,
-    ocean,
+    partner_ocean,
+    own_ocean,
     own_fields,
     partner_fields,
     ocean_adj,
@@ -105,7 +106,7 @@
 ):
     s = lax.axis_index("sfc")
     g = lax.axis_index("grp")
-    ocean_tiles = ocean.shape[1]
+    ocean_tiles = own_ocean.shape[0]
     atm_tiles = atm_hbm.shape[0]
     half_tiles = atm_tiles // 2
     tiles = weights.shape[0]
@@ -135,7 +136,12 @@
             barrier, inc=1, device_id={"sfc": sfc, "grp": grp}, device_id_type=MESH
         )
 
-    greet(s, 1 - g)
+    first = s == 0
+    unmet = jnp.logical_and(first, g == 1)
+
+    @pl.when(jnp.logical_not(jnp.logical_and(first, g == 0)))
+    def _():
+        greet(s, 1 - g)
 
     @pl.when(has_before)
     def _():
@@ -151,25 +157,18 @@
         local(target_hbm, target, 1),
         local(count_hbm, count, 2),
         local(ocean_adj_hbm, ocean_adj, 3),
-        local(ocean_hbm, ocean, 4),
+        local(ocean_hbm.at[1 - g], partner_ocean, 4),
     ]
+    ocean_copy = local(ocean_hbm.at[g], own_ocean, 9)
     weights_copy = local(weights_hbm, weights, 5)
     field_copy = local(atm_hbm, own_fields.at[0], 6)
     low_adj_copy = local(atm_adj_hbm.at[pl.ds(g * half_tiles, half_tiles)], atm_adj.at[0], 7)
     high_adj_copy = local(atm_adj_hbm.at[pl.ds(half_tiles, half_tiles)], atm_adj.at[1], 8)
-    for copy in small_copies + [weights_copy, field_copy, low_adj_copy]:
+    for copy in small_copies + [weights_copy]:
         copy.start()
 
-    @pl.when(g == 0)
-    def _():
-        high_adj_copy.start()
-
-    patient = jnp.logical_and(s == 0, g == 1)
-    prompt = jnp.logical_not(patient)
-
-    def meet():
-        peers = 1 + has_before.astype(jnp.int32) + 2 * sends_on.astype(jnp.int32)
-        pl.semaphore_wait(barrier, peers)
+    peers = 1 - unmet.astype(jnp.int32) + has_before.astype(jnp.int32)
+    pl.semaphore_wait(barrier, peers + 2 * sends_on.astype(jnp.int32))
 
     def partner_field(part):
         return remote(atm_hbm, partner_fields.at[0], 0, s, 1 - part)
@@ -181,27 +180,27 @@
     def before_adjacency():
         return remote(atm_adj_hbm.at[pl.ds(0, half_tiles)], atm_adj.at[1], 3, before, 1)
 
-    def send_fields():
-        @pl.when(g == 0)
-        def _():
-            partner_field(0).start()
-
-            @pl.when(has_before)
-            def _():
-                before_adjacency().start()
-
-        @pl.when(g == 1)
-        def _():
+    @pl.when(g == 0)
+    def _():
+        partner_field(0).start()
+
+        @pl.when(has_before)
+        def _():
+            before_adjacency().start()
+
+    @pl.when(g == 1)
+    def _():
+        @pl.when(has_before)
+        def _():
+            before_field(1).start()
             partner_field(1).start()
 
-            @pl.when(has_before)
-            def _():
-                before_field(1).start()
-
-    @pl.when(prompt)
-    def _():
-        meet()
-        send_fields()
+    for copy in [ocean_copy, field_copy, low_adj_copy]:
+        copy.start()
+
+    @pl.when(g == 0)
+    def _():
+        high_adj_copy.start()
 
     for copy in small_copies:
         copy.wait()
@@ -220,7 +219,7 @@
             places[t] = jnp.where(t < live, block_of(t), -2) - upper
 
     def scatter(out, part, first_tile, number):
-        group = 4
+        group = 16
 
         def step(i, carry):
             sums = [jnp.zeros((ROWS, LANES), F32) for _ in range(group)]
@@ -235,39 +234,41 @@
 
         lax.fori_loop(0, number // group, step, 0)
 
-    def pick_ocean(part, group):
+    def pick_ocean(ocean, group):
         for t in group:
-            got[t] = pick_lanes(lambda k: ocean[part, k], ocean_tiles, ocean_links[source[t]])
+            got[t] = pick_lanes(lambda k: ocean[k], ocean_tiles, ocean_links[source[t]])
 
         for t in group:
             block = source[t]
-            tile = ocean[part, block >> 1]
+            tile = ocean[block >> 1]
             field = jnp.where(upper * 0 + (block & 1) == 0, tile, roll_half(tile))
             slope = roll_half(got[t]) - got[t]
             picked[t, : 2 * ROWS] = stacked(jnp.where(lower_lanes(ROWS), field, slope))
 
     def forward(group):
-        for t in group:
+        for t in group[::2]:
             product = lax.dot_general(
-                picked[t, : 2 * ROWS],
-                split_weights[t],
+                jnp.concatenate([picked[t, : 2 * ROWS], picked[t + 1, : 2 * ROWS]], axis=0),
+                jnp.concatenate([split_weights[t], split_weights[t + 1]], axis=0),
                 (((1,), (1,)), ((), ())),
                 preferred_element_type=F32,
             )
-            added = product[:ROWS] + product[ROWS:]
-            terms[t] = added + roll_half(added)
+            for j in range(2):
+                mine = product[2 * ROWS * j : 2 * ROWS * (j + 1), LANES * j : LANES * (j + 1)]
+                added = mine[:ROWS] + mine[ROWS:]
+                terms[t + j] = added + roll_half(added)
 
     run_start = g * half_tiles * 2
     store_links(ocean_links, 0, ocean_adj, ocean_tiles)
-    store_places(lambda t: target[t] - run_start)
-    weights_copy.wait()
     group_size = 24
     groups = [range(i, i + group_size) for i in range(0, tiles, group_size)]
     for group in groups:
-        pick_ocean(1 - g, group)
+        pick_ocean(partner_ocean, group)
+        weights_copy.wait()
         for t in group:
             split_weights[t] = stacked(weights[t])
         forward(group)
+    store_places(lambda t: target[t] - run_start)
     scatter(partial, 0, 0, half_tiles)
 
     low_half, high_half = pl.ds(0, half_tiles), pl.ds(half_tiles, half_tiles)
@@ -281,37 +282,37 @@
     def partner_high():
         return remote(partial.at[0, high_half], from_partner.at[high_half], 7, s, 1)
 
-    def send_low():
-        for part in range(2):
-            pl.when(g == part)(partner_low(part).start)
-
-    pl.when(prompt)(send_low)
+    @pl.when(g == 0)
+    def _():
+        partner_low(0).start()
+
+    @pl.when(jnp.logical_and(g == 1, has_before))
+    def _():
+        partner_low(1).start()
+
     scatter(partial, 0, half_tiles, half_tiles)
 
-    def send_high():
-        @pl.when(g == 0)
-        def _():
-            partner_high().start()
-
-            @pl.when(has_before)
-            def _():
-                before_field(0).start()
-
-        @pl.when(sends_on)
-        def _():
-            following_sum(0).start()
-
-    def send_own_columns():
-        @pl.when(sends_on)
-        def _():
-            following_sum(1).start()
-
-    pl.when(prompt)(send_high)
+    @pl.when(g == 0)
+    def _():
+        partner_high().start()
+
+        @pl.when(has_before)
+        def _():
+            before_field(0).start()
+
+    @pl.when(sends_on)
+    def _():
+        following_sum(0).start()
+
+    ocean_copy.wait()
     for group in groups:
-        pick_ocean(g, group)
+        pick_ocean(own_ocean, group)
         forward(group)
     scatter(partial, 1, 0, atm_tiles)
-    pl.when(prompt)(send_own_columns)
+
+    @pl.when(sends_on)
+    def _():
+        following_sum(1).start()
 
     is_last = jnp.logical_not(has_following).astype(jnp.int32)
 
@@ -371,14 +372,6 @@
     backward()
     scatter(ocean_out, g, 0, ocean_tiles)
 
-    @pl.when(patient)
-    def _():
-        meet()
-        send_fields()
-        send_low()
-        send_high()
-        send_own_columns()
-
     @pl.when(g == 0)
     def _():
         partner_field(1).wait_recv()
@@ -386,6 +379,11 @@
     @pl.when(g == 1)
     def _():
         partner_field(0).wait_recv()
+
+        @pl.when(first)
+        def _():
+            partner_field(1).start()
+            partner_low(1).start()
 
     @pl.when(sends_on)
     def _():
@@ -506,7 +504,8 @@
         in_specs=[pl.BlockSpec(memory_space=pltpu.HBM)] * 8,
         out_specs=(vmem, vmem),
         scratch_shapes=[
-            pltpu.VMEM((2, ocean_tiles, ROWS, LANES), F32),
+            pltpu.VMEM((ocean_tiles, ROWS, LANES), F32),
+            pltpu.VMEM((ocean_tiles, ROWS, LANES), F32),
             pltpu.VMEM((2, atm_tiles, ROWS, LANES), F32),
             pltpu.VMEM((2, atm_tiles, ROWS, LANES), F32),
             pltpu.VMEM((ocean_tiles, 2, LANES), jnp.int32),
@@ -525,7 +524,7 @@
             pltpu.VMEM((2, atm_tiles, ROWS, LANES), F32),
             pltpu.VMEM((atm_tiles, ROWS, LANES), F32),
             pltpu.VMEM((half_tiles, ROWS, LANES), F32),
-            pltpu.SemaphoreType.DMA((9,)),
+            pltpu.SemaphoreType.DMA((10,)),
             pltpu.SemaphoreType.DMA((8,)),
             pltpu.SemaphoreType.DMA((8,)),
         ],

time: 17 us -> 16.6 us (0.976)
  Pallas kernels: 15.5 us -> 15.2 us
    pallas_call x1, Pallas kernels: 14.8 us -> 14.5 us  [per_device(): pl.pallas_call(functools.partial(kernel, n_sfc), out_shape=(pltpu.VMEM((a...]
where the time goes in v5:
time: 16.6 us; the launch traced here: 16.5 us
  Pallas kernels  15.2 us (92%)
  between operations  1.29 us (8%)
    pallas_call x1, Pallas kernels, per_device(): pl.pallas_call(functools.partial(kernel, n_sfc), out_shape=(pltpu.VMEM((a...  14.5 us
    pallas_call x1, Pallas kernels, write_out(): pl.pallas_call(write_kernel, out_shape=(jax.ShapeDtypeStruct(atm.shape, F...  0.72 us

profile of v5, /device:TPU:1, one launch (start us, length us, event | category | flops | bytes accessed | tf_op | source)
XLA Modules:
  0.0 16.5 jit_solution(7686997383403815911)
XLA Ops:
  1.3 14.5 %shard_map.95 = (f32[32,8,128]{2,1,0:T(8,128)S(1)}, f32[2,16,8,128]{3,2,1,0:T(8,128)S(1)}) custom-call(f32[2,16,8,128]{3,2,1,0:T(8,128)} %bitcast.18, f32[32,8,128]{2,1,0:T(8,128)} %bitcast.19, f32[24,64,128]{2,1,0:T(8,128)} %weights_hbm.1, s32[24]{0:T(128)} %source_hbm.1, s32[24]{0:T(128)} %target_hbm.1, s32[1]{0:T(128)S(6)} %copy.10.count_hbm, ...), custom_call_target="tpu_custom_call" | custom-call | tf_op jit(solution)/shard_map/pallas_call | solution.py:498
  15.8 0.7 %shard_map.96 = (f32[32,8,128]{2,1,0:T(8,128)}, f32[2,16,8,128]{3,2,1,0:T(8,128)}) custom-call(f32[32,8,128]{2,1,0:T(8,128)S(1)} %get-tuple-element.6.atm, f32[2,16,8,128]{3,2,1,0:T(8,128)S(1)} %get-tuple-element.7.ocean), custom_call_target="tpu_custom_call" | custom-call | tf_op jit(solution)/shard_map/pallas_call | solution.py:465

commit v6 on v5

--- a/solution.py
+++ b/solution.py
@@ -219,7 +219,7 @@
             places[t] = jnp.where(t < live, block_of(t), -2) - upper
 
     def scatter(out, part, first_tile, number):
-        group = 16
+        group = number
 
         def step(i, carry):
             sums = [jnp.zeros((ROWS, LANES), F32) for _ in range(group)]
@@ -346,12 +346,18 @@
 
     def backward():
         lower = lower_lanes(ROWS)
-        for t in range(tiles):
-            product = jnp.dot(picked[t], split_weights[t], preferred_element_type=F32)
-            field = product[:ROWS] + product[ROWS : 2 * ROWS]
-            slope = product[2 * ROWS : 3 * ROWS] + product[3 * ROWS :]
-            both = jnp.where(lower, field, slope)
-            terms[t] = both + roll_half(both)
+        for t in range(0, tiles, 2):
+            product = jnp.dot(
+                jnp.concatenate([picked[t], picked[t + 1]], axis=0),
+                jnp.concatenate([split_weights[t], split_weights[t + 1]], axis=1),
+                preferred_element_type=F32,
+            )
+            for j in range(2):
+                mine = product[4 * ROWS * j : 4 * ROWS * (j + 1), LANES * j : LANES * (j + 1)]
+                field = mine[:ROWS] + mine[ROWS : 2 * ROWS]
+                slope = mine[2 * ROWS : 3 * ROWS] + mine[3 * ROWS :]
+                both = jnp.where(lower, field, slope)
+                terms[t + j] = both + roll_half(both)
 
     low_adj_copy.wait()
     field_copy.wait()

time: 16.6 us -> 16.7 us (level)
  no operation moved by 1% of the time
where the time goes in v6:
time: 16.7 us; the launch traced here: 16.5 us
  Pallas kernels  15.2 us (91%)
  between operations  1.29 us (8%)
    pallas_call x1, Pallas kernels, per_device(): pl.pallas_call(functools.partial(kernel, n_sfc), out_shape=(pltpu.VMEM((a...  14.5 us
    pallas_call x1, Pallas kernels, write_out(): pl.pallas_call(write_kernel, out_shape=(jax.ShapeDtypeStruct(atm.shape, F...  0.72 us

profile of v6, /device:TPU:1, one launch (start us, length us, event | category | flops | bytes accessed | tf_op | source)
XLA Modules:
  0.0 16.5 jit_solution(15516626924277691844)
XLA Ops:
  1.3 14.5 %shard_map.95 = (f32[32,8,128]{2,1,0:T(8,128)S(1)}, f32[2,16,8,128]{3,2,1,0:T(8,128)S(1)}) custom-call(f32[2,16,8,128]{3,2,1,0:T(8,128)} %bitcast.18, f32[32,8,128]{2,1,0:T(8,128)} %bitcast.19, f32[24,64,128]{2,1,0:T(8,128)} %weights_hbm.1, s32[24]{0:T(128)} %source_hbm.1, s32[24]{0:T(128)} %target_hbm.1, s32[1]{0:T(128)S(6)} %copy.10.count_hbm, ...), custom_call_target="tpu_custom_call" | custom-call | tf_op jit(solution)/shard_map/pallas_call | solution.py:504
  15.8 0.7 %shard_map.96 = (f32[32,8,128]{2,1,0:T(8,128)}, f32[2,16,8,128]{3,2,1,0:T(8,128)}) custom-call(f32[32,8,128]{2,1,0:T(8,128)S(1)} %get-tuple-element.6.atm, f32[2,16,8,128]{3,2,1,0:T(8,128)S(1)} %get-tuple-element.7.ocean), custom_call_target="tpu_custom_call" | custom-call | tf_op jit(solution)/shard_map/pallas_call | solution.py:471
